TPU v7x, 32 devices: a whole 2x2x4 slice. The times are simulated.
32 devices in a mesh: rows: 8 (over y, x, core), mlp: 4 (over z).
Axes of the slice: x: 2, y: 2, z: 4, core: 2. Of those that a mesh axis runs over, the one named last changes fastest.
Arguments:
- patches: bfloat16 [18576, 768], P('rows'), may hold values from -6 to 6
- w_qkv: bfloat16 [768, 2304], P(None, 'mlp'), may hold values from -0.3125 to 0.3125
- qkv_bias: float32 [2, 768], replicated, may hold values from -2 to 2
- w_out: bfloat16 [768, 768], P('mlp'), may hold values from -0.875 to 0.875
- post_bias: float32 [2, 768], replicated, may hold values from -2 to 2
- w_up: bfloat16 [768, 3072], P(None, 'mlp'), may hold values from -0.21875 to 0.21875
- up_bias: float32 [3072], P('mlp'), may hold values from -2 to 2
- w_down: bfloat16 [3072, 768], P('mlp'), may hold values from -0.15625 to 0.15625
- norm_gains: float32 [2, 768], replicated, may hold values from 0.5 to 1.5
- norm_shifts: float32 [2, 768], replicated, may hold values from -2 to 2
- router: float32 [768], replicated, may hold values from -0.21875 to 0.21875
- picked: int32 [11688], P('rows'), may hold values from 0 to 2321, as said below
- live_slots: int32 [11688], P('rows'), may hold values from 0 to 1, as said below
- cotangent: bfloat16 [18576, 768], P('rows', 'mlp'), may hold values from -6 to 6
Outputs:
- block_out: bfloat16 [18576, 768], P('rows', 'mlp')
- input_grad: bfloat16 [18576, 768], P('rows')
- d_qkv: float32 [768, 2304], P(None, 'mlp')
- d_qkv_bias: float32 [2, 768], P(None, 'mlp')
- d_out: float32 [768, 768], P('mlp')
- d_post_bias: float32 [2, 768], replicated
- d_up: float32 [768, 3072], P(None, 'mlp')
- d_up_bias: float32 [3072], P('mlp')
- d_down: float32 [3072, 768], P('mlp')
- d_gains: float32 [2, 768], replicated
- d_shifts: float32 [2, 768], replicated
- d_router: float32 [768], replicated
Inputs may be any that keep to these rules, and one draw needn't show every extreme that they name: `picked`: in each group, slot s < 594 belongs to small image s // 99 and a later slot to large image (s - 594) // 289. The live slots of one image name distinct rows in rising order, all within one run of 197 (small) or 577 (large) rows that holds that image and no other; no row is named by two live slots; slots that are not live name the group's last row. `live_slots`: constant over each image's slots. In each group the live images are the first n large ones and the first 6 - n small ones, 0 <= n <= 3; some group has n = 0 and another n = 3.
All inputs are finite; a program needn't handle non-finite values.
Results may differ from a plain program's by a relative error of at most 0.013.
The roundings to bfloat16 on the way count: a program that leaves them out, or rounds other values in their place, can miss the bound.
Values may be sent and summed in bfloat16 or wider, within the bound.
No kernel may reach another device: no remote copies, remote signals or barrier semaphores. Data moves between devices by JAX's collectives and lax.ppermute only.
A program may use at most 256 MiB of HBM per device.

v0:
```python
import jax
import jax.numpy as jnp
from jax import lax
from jax.sharding import PartitionSpec as P

HD = 64
IMG_DEV = 6
L_MOST = 3
HALF_S = 99
HALF_L = 289


HIGH = lax.Precision.HIGHEST
EPSILON = 1e-06
LOWER = jnp.bfloat16
FLOAT = jnp.float32


def norm_forward(values, norm_gain, norm_shift):
    average = jnp.mean(values, axis=-1, keepdims=True)
    centred = values - average
    variance = jnp.mean(centred * centred, axis=-1, keepdims=True)
    inverse = lax.rsqrt(variance + EPSILON)
    scaled = centred * inverse
    return (scaled * norm_gain + norm_shift, scaled, inverse)


def norm_backward(grad_out, scaled, inverse, norm_gain):
    gain_grad = jnp.sum(grad_out * scaled, axis=0)
    shift_grad = jnp.sum(grad_out, axis=0)
    weighted = grad_out * norm_gain
    centre_term = jnp.mean(weighted, axis=-1, keepdims=True)
    scale_term = jnp.mean(weighted * scaled, axis=-1, keepdims=True)
    return (inverse * (weighted - centre_term - scaled * scale_term), gain_grad, shift_grad)


def split_heads(projected, images, length, head_count):
    shaped = projected.reshape(images, length, head_count, 3, HD)
    return (shaped[:, :, :, 0, :], shaped[:, :, :, 1, :], shaped[:, :, :, 2, :])


def attend_forward(projected, images, length, head_count, score_scale):
    queries, keys, values = split_heads(projected, images, length, head_count)
    scores = (
        jnp.einsum("blhd,bmhd->bhlm", queries, keys, preferred_element_type=FLOAT) * score_scale
    )
    largest = jnp.max(scores, axis=-1, keepdims=True)
    powered = jnp.exp(scores - largest)
    total = jnp.sum(powered, axis=-1, keepdims=True)
    probs = powered / total
    mixed = jnp.einsum("bhlm,bmhd->blhd", probs.astype(LOWER), values, preferred_element_type=FLOAT)
    return (mixed.reshape(images * length, head_count * HD), largest + jnp.log(total))


def attend_backward(projected, log_total, grad_mix, images, length, head_count, score_scale):
    queries, keys, values = split_heads(projected, images, length, head_count)
    grad_heads = grad_mix.reshape(images, length, head_count, HD)
    scores = (
        jnp.einsum("blhd,bmhd->bhlm", queries, keys, preferred_element_type=FLOAT) * score_scale
    )
    probs = jnp.exp(scores - log_total)
    grad_probs = jnp.einsum("blhd,bmhd->bhlm", grad_heads, values, preferred_element_type=FLOAT)
    inner = jnp.sum(probs * grad_probs, axis=-1, keepdims=True)
    grad_scores = (probs * (grad_probs - inner)).astype(LOWER)
    grad_queries = (
        jnp.einsum("bhlm,bmhd->blhd", grad_scores, keys, preferred_element_type=FLOAT) * score_scale
    )
    grad_keys = (
        jnp.einsum("bhlm,blhd->bmhd", grad_scores, queries, preferred_element_type=FLOAT)
        * score_scale
    )
    grad_values = jnp.einsum(
        "bhlm,blhd->bmhd", probs.astype(LOWER), grad_heads, preferred_element_type=FLOAT
    )
    stacked = jnp.stack([grad_queries, grad_keys, grad_values], axis=3)
    return stacked.reshape(images * length, head_count * 3 * HD)


def local(
    patches,
    w_qkv,
    qkv_bias,
    w_out,
    post_bias,
    w_up,
    up_bias,
    w_down,
    norm_gains,
    norm_shifts,
    router,
    picked,
    live_slots,
    cotangent,
):
    model_width = patches.shape[1]
    mlp_index = lax.axis_index("mlp")
    slice_cols = w_qkv.shape[1]
    own_width = w_out.shape[0]
    feature_slice = cotangent.shape[1]
    heads_here = own_width // HD
    score_scale = HD ** (-0.5)
    small_slots = IMG_DEV * HALF_S
    live_float = live_slots.astype(FLOAT)[:, None]
    picked_rows = patches[picked].astype(FLOAT)
    gate_value = jax.nn.sigmoid(jnp.dot(picked_rows, router, precision=HIGH))
    normed_one, scaled_one, inverse_one = norm_forward(picked_rows, norm_gains[0], norm_shifts[0])
    normed_one = normed_one.astype(LOWER)
    bias_rows = jnp.stack([qkv_bias[0], jnp.zeros_like(qkv_bias[0]), qkv_bias[1]])
    bias_cols = (
        bias_rows.reshape(3, model_width // HD, HD).transpose(1, 0, 2).reshape(3 * model_width)
    )
    head_qkv, head_out = (
        lax.all_gather(w_qkv, "mlp", axis=1, tiled=True),
        lax.all_gather(w_out, "mlp", axis=0, tiled=True),
    )
    head_count = model_width // HD
    projected = (jnp.dot(normed_one, head_qkv, preferred_element_type=FLOAT) + bias_cols).astype(
        LOWER
    )
    small_mix, small_total = attend_forward(
        projected[:small_slots], IMG_DEV, HALF_S, head_count, score_scale
    )
    large_mix, large_total = attend_forward(
        projected[small_slots:], L_MOST, HALF_L, head_count, score_scale
    )
    head_mix = jnp.concatenate([small_mix, large_mix], axis=0).astype(LOWER)
    attn_term = jnp.dot(head_mix, head_out, preferred_element_type=FLOAT)
    attn_out = attn_term + post_bias[0]
    hidden = picked_rows + attn_out
    normed_two, scaled_two, inverse_two = norm_forward(hidden, norm_gains[1], norm_shifts[1])
    normed_two = normed_two.astype(LOWER)
    pre_act = jnp.dot(normed_two, w_up, preferred_element_type=FLOAT) + up_bias
    activation = jax.nn.gelu(pre_act, approximate=False).astype(LOWER)
    mlp_term = lax.psum_scatter(
        jnp.dot(activation, w_down, preferred_element_type=FLOAT).astype(jnp.bfloat16),
        "mlp",
        scatter_dimension=1,
        tiled=True,
    ).astype(jnp.float32)
    feature_start = mlp_index * feature_slice
    mlp_slice = mlp_term + lax.dynamic_slice_in_dim(post_bias[1], feature_start, feature_slice)
    attn_slice = lax.dynamic_slice_in_dim(attn_out, feature_start, feature_slice, 1)
    patch_slice = lax.dynamic_slice_in_dim(patches, feature_start, feature_slice, 1).astype(FLOAT)
    branch = gate_value[:, None] * (attn_slice + mlp_slice) * live_float
    block_out = patch_slice.at[picked].add(branch).astype(LOWER)
    full_cot = lax.all_gather(cotangent, "mlp", axis=1, tiled=True).astype(FLOAT)
    cot_rows = full_cot[picked] * live_float
    gated = gate_value[:, None] * cot_rows
    grad_mlp = gated.astype(LOWER)
    d_down = jnp.einsum("pf,pd->fd", activation, grad_mlp, preferred_element_type=FLOAT)
    d_down_bias = jnp.sum(gated, axis=0)
    grad_act = jnp.einsum("pd,fd->pf", grad_mlp, w_down, preferred_element_type=FLOAT)
    gelu_pull = jax.vjp(lambda inner_value: jax.nn.gelu(inner_value, approximate=False), pre_act)[1]
    grad_pre = gelu_pull(grad_act)[0].astype(LOWER)
    d_up = jnp.einsum("pd,pf->df", normed_two, grad_pre, preferred_element_type=FLOAT)
    d_up_bias = jnp.sum(grad_pre.astype(FLOAT), axis=0)
    norm_two_part = jnp.einsum("pf,df->pd", grad_pre, w_up, preferred_element_type=FLOAT)
    cot_slice = lax.dynamic_slice_in_dim(cot_rows, feature_start, feature_slice, 1)
    gate_part = jnp.sum(cot_slice * mlp_slice, axis=1)
    grad_normed_two, gate_sum = lax.psum((norm_two_part, gate_part), "mlp")
    grad_gate = jnp.sum(cot_rows * attn_out, axis=1) + gate_sum
    grad_hidden, d_gain_two, d_shift_two = norm_backward(
        grad_normed_two, scaled_two, inverse_two, norm_gains[1]
    )
    grad_attn = grad_hidden + gated
    d_out_bias = jnp.sum(grad_attn, axis=0)
    grad_attn_low = grad_attn.astype(LOWER)
    own_mix = lax.dynamic_slice_in_dim(head_mix, mlp_index * own_width, own_width, 1)
    d_out = jnp.einsum("pk,pd->kd", own_mix, grad_attn_low, preferred_element_type=FLOAT)
    grad_mix = jnp.einsum(
        "pd,kd->pk", grad_attn_low, head_out, preferred_element_type=FLOAT
    ).astype(LOWER)
    small_grad = attend_backward(
        projected[:small_slots],
        small_total,
        grad_mix[:small_slots],
        IMG_DEV,
        HALF_S,
        head_count,
        score_scale,
    )
    large_grad = attend_backward(
        projected[small_slots:],
        large_total,
        grad_mix[small_slots:],
        L_MOST,
        HALF_L,
        head_count,
        score_scale,
    )
    grad_proj = jnp.concatenate([small_grad, large_grad], axis=0).astype(LOWER)
    own_proj = lax.dynamic_slice_in_dim(grad_proj, mlp_index * slice_cols, slice_cols, 1)
    grad_normed_one = jnp.einsum("pc,dc->pd", grad_proj, head_qkv, preferred_element_type=FLOAT)
    d_qkv = jnp.einsum("pd,pc->dc", normed_one, own_proj, preferred_element_type=FLOAT)
    bias_grad = jnp.sum(own_proj.astype(FLOAT), axis=0).reshape(heads_here, 3, HD)
    d_qkv_bias = jnp.stack(
        [bias_grad[:, 0, :].reshape(own_width), bias_grad[:, 2, :].reshape(own_width)]
    )
    grad_norm_rows, d_gain_one, d_shift_one = norm_backward(
        grad_normed_one, scaled_one, inverse_one, norm_gains[0]
    )
    grad_logit = grad_gate * gate_value * (1.0 - gate_value)
    d_router = jnp.dot(grad_logit, picked_rows, precision=HIGH)
    grad_rows = (grad_hidden + grad_norm_rows + grad_logit[:, None] * router[None, :]) * live_float
    input_grad = full_cot.at[picked].add(grad_rows).astype(LOWER)
    (
        d_qkv,
        d_qkv_bias,
        d_out,
        d_out_bias,
        d_gain_one,
        d_shift_one,
        d_router,
        d_up,
        d_up_bias,
        d_down,
        d_gain_two,
        d_shift_two,
        d_down_bias,
    ) = lax.psum(
        (
            d_qkv,
            d_qkv_bias,
            d_out,
            d_out_bias,
            d_gain_one,
            d_shift_one,
            d_router,
            d_up,
            d_up_bias,
            d_down,
            d_gain_two,
            d_shift_two,
            d_down_bias,
        ),
        "rows",
    )
    d_gains = jnp.stack([d_gain_one, d_gain_two])
    d_shifts = jnp.stack([d_shift_one, d_shift_two])
    d_post_bias = jnp.stack([d_out_bias, d_down_bias])
    return (
        block_out,
        input_grad,
        d_qkv,
        d_qkv_bias,
        d_out,
        d_post_bias,
        d_up,
        d_up_bias,
        d_down,
        d_gains,
        d_shifts,
        d_router,
    )


def solution(mesh):
    in_specs = (
        P("rows", None),
        P(None, "mlp"),
        P(),
        P("mlp", None),
        P(),
        P(None, "mlp"),
        P("mlp"),
        P("mlp", None),
        P(),
        P(),
        P(),
        P("rows"),
        P("rows"),
        P("rows", "mlp"),
    )
    out_specs = (
        P("rows", "mlp"),
        P("rows", None),
        P(None, "mlp"),
        P(None, "mlp"),
        P("mlp", None),
        P(),
        P(None, "mlp"),
        P("mlp"),
        P("mlp", None),
        P(),
        P(),
        P(),
    )
    return jax.shard_map(local, mesh=mesh, in_specs=in_specs, out_specs=out_specs, check_vma=False)
```

profile of v0, /device:TPU:0, one launch (start us, length us, event | category | flops | bytes accessed | tf_op | source)
XLA Modules:
  0.0 767.8 jit_solution(8699501108456615047)
XLA Ops:
  26.7 55.6 %all-gather.4.cloned.1.call-done = bf16[768,2304]{0,1:T(8,128)(2,1)} async-done(((bf16[768,576]{0,1:T(8,128)(2,1)}), bf16[768,2304]{0,1:T(8,128)(2,1)}) %all-gather.4.cloned.1.call-update) | async-done | bytes 3538960 | tf_op jit(solution)/shard_map/all_gather | solution.py:113
  95.2 14.3 %reshape.182 = bf16[6,99,12,3,64]{4,3,2,1,0:T(4,128)(2,1)} reshape(bf16[594,2304]{1,0:T(8,128)(2,1)} %slice.94) | data formatting | bytes 5474304 | tf_op jit(solution)/shard_map/reshape | solution.py:38
  109.4 17.4 %fusion.120 = (bf16[6,99,12,1,64]{4,3,2,1,0:T(2,128)(2,1)}, bf16[6,99,12,1,64]{4,3,2,1,0:T(2,128)(2,1)}, bf16[6,99,12,1,64]{4,3,2,1,0:T(2,128)(2,1)}) fusion(bf16[6,99,12,3,64]{4,3,2,1,0:T(4,128)(2,1)} %reshape.182), kind=kLoop, calls=%fused_computation.196 | loop fusion | bytes 5474304 | tf_op jit(solution)/shard_map/slice | solution.py:39
  162.9 20.0 %reshape.183 = bf16[3,289,12,3,64]{4,3,2,1,0:T(4,128)(2,1)} reshape(bf16[867,2304]{1,0:T(8,128)(2,1)} %slice.98) | data formatting | bytes 7990272 | tf_op jit(solution)/shard_map/reshape | solution.py:38
  182.9 22.8 %fusion.119 = (bf16[3,289,12,1,64]{4,3,2,1,0:T(2,128)(2,1)}, bf16[3,289,12,1,64]{4,3,2,1,0:T(2,128)(2,1)}, bf16[3,289,12,1,64]{4,3,2,1,0:T(2,128)(2,1)}) fusion(bf16[3,289,12,3,64]{4,3,2,1,0:T(4,128)(2,1)} %reshape.183), kind=kLoop, calls=%fused_computation.195 | loop fusion | bytes 7990272 | tf_op jit(solution)/shard_map/slice | solution.py:39
  205.7 11.8 %copy.128 = bf16[3,289,12,1,64]{1,4,2,0,3:T(8,128)(2,1)} copy(bf16[3,289,12,1,64]{4,3,2,1,0:T(2,128)(2,1)} %get-tuple-element.74) | data formatting | bytes 2663424
  217.5 11.8 %copy.129 = bf16[3,289,12,1,64]{1,4,2,0,3:T(8,128)(2,1)} copy(bf16[3,289,12,1,64]{4,3,2,1,0:T(2,128)(2,1)} %get-tuple-element.75) | data formatting | bytes 2663424
  229.3 12.2 %copy.130 = bf16[3,289,12,1,64]{1,4,2,0,3:T(8,128)(2,1)} copy(bf16[3,289,12,1,64]{4,3,2,1,0:T(2,128)(2,1)} %get-tuple-element.76) | data formatting | bytes 2663424
  241.6 10.7 %multiply_reduce_fusion.1 = (f32[3,12,289]{2,1,0:T(8,128)S(1)}, f32[3,12,289,289]{2,3,1,0:T(8,128)}) fusion(bf16[3,289,12,1,64]{1,4,2,0,3:T(8,128)(2,1)} %copy.130, bf16[3,289,12,1,64]{1,4,2,0,3:T(8,128)(2,1)} %copy.129), kind=kOutput, calls=%fused_computation.11 | convolution fusion | flops 390867872 | bytes 14732064 | tf_op jit(solution)/shard_map/blhd,bmhd->bhlm/dot_general | solution.py:45
  261.3 9.6 %convert_bitcast_fusion.1 = bf16[3,289,12,64]{1,3,2,0:T(8,128)(2,1)S(1)} fusion(f32[3,12,289,289]{2,3,1,0:T(8,128)} %get-tuple-element.89, f32[3,12,289]{2,1,0:T(8,128)S(1)} %fusion, f32[3,12,289]{2,1,0:T(8,128)S(1)} %get-tuple-element.88, bf16[3,289,12,1,64]{1,4,2,0,3:T(8,128)(2,1)S(1)} %copy-done.13), kind=kOutput, calls=%fused_computation.120 | convolution fusion | flops 397557632 | bytes 14773680 | tf_op jit(solution)/shard_map/bhlm,bmhd->blhd/dot_general | solution.py:51
  290.7 9.7 %gather_fusion.1 = f32[1461,768]{1,0:T(8,128)} fusion(f32[2322,768]{1,0:T(8,128)} %convert_element_type.86, s32[2048]{0:T(1024)S(1)} %pad_clamp_fusion), kind=kCustom, calls=%fused_computation.1 | custom fusion | bytes 8982228 | tf_op jit(solution)/shard_map/gather | solution.py:147
  300.4 9.8 %multiply_reduce_fusion.8 = (f32[768]{0:T(1024)}, f32[1461]{0:T(1024)}, f32[1461,768]{1,0:T(8,128)S(1)}, f32[1461]{0:T(1024)S(1)}, f32[1461,768]{1,0:T(8,128)S(1)}, /*index=5*/f32[1461,768]{1,0:T(8,128)}) fusion(f32[1461]{0:T(1024)S(1)} %add_divide_fusion, f32[1461,768]{1,0:T(8,128)} %gather_fusion.1, f32[1461]{0:T(1024)S(1)} %convert_element_type.84, ...), kind=kOutput, calls=%fused_computation.73 | convolution fusion | flops 1738048768 | bytes 23650128 | tf_op jit(solution)/shard_map/dot_general | solution.py:127
  312.2 13.1 %multiply_convert_fusion.1 = (bf16[1461,768]{1,0:T(8,128)(2,1)}, f32[1461,768]{1,0:T(8,128)S(1)}, f32[1461,768]{1,0:T(8,128)S(1)}) fusion(f32[768]{0:T(1024)S(1)} %copy-done.70, bf16[1461,768]{1,0:T(8,128)(2,1)S(1)} %add_convert_fusion.1, bf16[768,768]{1,0:T(8,128)(2,1)S(1)} %copy-done), kind=kOutput, calls=%fused_computation.53 | convolution fusion | flops 1797520896 | bytes 14647296 | tf_op jit(solution)/shard_map/dot_general | solution.py:132
  357.4 141.5 %all-reduce.5.cloned.1.call-done = f32[1461,768]{1,0:T(8,128)} async-done(((f32[1461,768]{1,0:T(8,128)}), f32[1461,768]{1,0:T(8,128)}) %all-reduce.5.cloned.1.call-update) | async-done | bytes 4488208 | tf_op jit(solution)/shard_map/psum | solution.py:160
  541.0 15.9 %multiply_reduce_fusion = (f32[3,12,289]{2,1,0:T(8,128)S(1)}, f32[3,12,289,289]{2,3,1,0:T(8,128)}) fusion(f32[3,12,289,289]{2,3,1,0:T(8,128)} %get-tuple-element.89, f32[3,12,289]{2,1,0:T(8,128)S(1)} %log_add_fusion, bf16[3,289,12,64]{1,3,2,0:T(8,128)(2,1)S(1)} %copy.100, bf16[3,289,12,1,64]{1,4,2,0,3:T(8,128)(2,1)} %copy.128), kind=kOutput, calls=%fused_computation.5 | convolution fusion | flops 396881376 | bytes 26800704 | tf_op jit(solution)/shard_map/blhd,bmhd->bhlm/dot_general | solution.py:62
  574.4 11.7 %multiply_convert_fusion = bf16[3,12,289,289]{2,3,1,0:T(8,128)(2,1)S(1)} fusion(f32[3,12,289,289]{2,3,1,0:T(8,128)} %get-tuple-element.95, f32[3,12,289,289]{2,3,1,0:T(8,128)} %get-tuple-element.89, f32[3,12,289]{2,1,0:T(8,128)S(1)} %get-tuple-element.94, f32[3,12,289]{2,1,0:T(8,128)S(1)} %log_add_fusion), kind=kLoop, calls=%fused_computation.4 | loop fusion | flops 15033780 | bytes 30150792 | tf_op jit(solution)/shard_map/convert_element_type | solution.py:64
  593.0 9.8 %convert_bitcast_fusion = bf16[3,289,12,1,64]{1,4,2,0,3:T(8,128)(2,1)} fusion(bf16[3,289,12,64]{1,3,2,0:T(8,128)(2,1)S(1)} %copy.100, f32[3,12,289,289]{2,3,1,0:T(8,128)} %get-tuple-element.89, f32[3,12,289]{2,1,0:T(8,128)S(1)} %log_add_fusion), kind=kOutput, calls=%fused_computation.119 | convolution fusion | flops 394550880 | bytes 14732064 | tf_op jit(solution)/shard_map/bhlm,blhd->bmhd/dot_general | solution.py:72
  610.5 10.4 %copy.105 = bf16[3,289,12,3,64]{1,0,4,3,2:T(4,128)(2,1)} copy(bf16[3,289,12,3,64]{1,4,2,0,3:T(8,128)(2,1)} %pad_maximum_fusion.2) | data formatting | bytes 7990272 | tf_op jit(solution)/shard_map/stack | solution.py:75
  620.9 13.4 %reshape.138 = bf16[867,2304]{0,1:T(8,128)(2,1)} reshape(bf16[3,289,12,3,64]{1,0,4,3,2:T(4,128)(2,1)} %copy.105) | data formatting | bytes 7990272 | tf_op jit(solution)/shard_map/reshape | solution.py:76
  643.3 15.6 %scatter_custom_fusion = f32[2322,192]{1,0:T(8,128)} fusion(f32[2322,192]{1,0:T(8,128)} %dynamic-slice_convert_fusion, s32[1461]{0:T(1024)} %copy-done.54, bf16[1461,192]{1,0:T(8,128)(2,1)S(1)} %copy.116, f32[1461,768]{1,0:T(8,128)} %get-tuple-element.90, s32[]{:T(128)} %constant.42.clone.1, s32[]{:T(128)S(6)} %select_n.6, f32[1461]{0:T(1024)S(1)} %copy-done.38, ...), kind=kCustom, calls=%fused_computation.126 | custom fusion | flops 1683072 | bytes 3856428 | tf_op jit(solution)/shard_map/scatter-add | solution.py:145
  672.6 13.5 %fusion.25 = (f32[768]{0:T(1024)S(1)}, f32[1461]{0:T(1024)S(1)}, f32[1461]{0:T(1024)S(1)}, f32[768]{0:T(1024)S(1)}, f32[1461,768]{1,0:T(8,128)}) fusion(bf16[1461,768]{1,0:T(8,128)(2,1)S(1)} %copy-done.4, f32[1461]{0:T(1024)S(1)} %copy-done.52, f32[1461]{0:T(1024)S(1)} %copy-done.44, f32[768]{0:T(1024)S(1)} %copy-done.56, ...), kind=kOutput, calls=%fused_computation.42 | convolution fusion | flops 5195079680 | bytes 17036112 | tf_op jit(solution)/shard_map/pc,dc->pd/dot_general | solution.py:193
  686.5 22.3 %scatter_custom_fusion.1 = f32[2322,768]{1,0:T(8,128)} fusion(f32[2322,768]{1,0:T(8,128)} %convert_element_type.86, s32[1461]{0:T(1024)} %copy-done.54, bf16[1461,768]{1,0:T(8,128)(2,1)S(1)} %copy-done.4, f32[1461,768]{1,0:T(8,128)} %get-tuple-element.96, f32[768]{0:T(1024)S(1)} %copy-done.57, f32[1461]{0:T(1024)S(1)} %subtract_multiply_fusion.2, ...), kind=kCustom, calls=%fused_computation.41 | custom fusion | flops 22440960 | bytes 22937160 | tf_op jit(solution)/shard_map/scatter-add | solution.py:205
  715.0 23.6 %all-reduce = (f32[2,192]{1,0:T(2,128)}, f32[1,768]{1,0:T(1,128)S(1)}, f32[1,768]{1,0:T(1,128)S(1)}, f32[768]{0:T(1024)}, f32[1,768]{1,0:T(1,128)S(1)}, /*index=...) all-reduce(f32[2,192]{1,0:T(2,128)S(1)} %pad_maximum_fusion.10, ...), channel_id=1, replica_groups=mesh['rows'=8,'mlp'=4] {'rows'}, use_global_device_ids=true, to_apply=%region_23.0 | all-reduce | flops 6528 | bytes 52224 | tf_op jit(solution)/shard_map/psum | solution.py:220
  740.4 12.5 %all-reduce.7.cloned.1.call-done = (f32[768,576]{0,1:T(8,128)}, f32[192,768]{1,0:T(8,128)}, f32[768,768]{1,0:T(8,128)}, f32[768,768]{1,0:T(8,128)}) async-done(((f32[768,576]{0,1:T(8,128)}, f32[192,768]{1,0:T(8,128)}, f32[768,768]{1,0:T(8,128)}, f32[768,768]{1,0:T(8,128)}), (f32[768,576]{0,1:T(8,128)}, f32[192,768]{1,0:T(8,128)}, f32[768,768]{1,0:T(8,128)}, ...) | async-done | bytes 7077904 | tf_op jit(solution)/shard_map/psum | solution.py:220
  (261 shorter events, 243.6 us)
Async XLA Ops:
  7.2 305.0 %copy-start = (bf16[768,768]{1,0:T(8,128)(2,1)S(1)}, bf16[768,768]{1,0:T(8,128)(2,1)}, u32[]{:S(2)}) copy-start(bf16[768,768]{1,0:T(8,128)(2,1)} %param.19) | copy-start | bytes 3538948
  7.2 75.1 %all-gather.4.cloned.1.call-start = ((), (), s32[]{:S(2)}) async-start(), calls=%async_computation.1 | async-start | bytes 4423680 | tf_op jit(solution)/shard_map/all_gather | solution.py:113
  7.9 271.1 %all-gather.8.cloned.1.call-start = ((), (), s32[]{:S(2)}) async-start(), calls=%async_computation.3 | async-start | bytes 4669440 | tf_op jit(solution)/shard_map/all_gather | solution.py:146
  8.7 291.7 %all-gather.6.cloned.1.call-start = ((), (), s32[]{:S(2)}) async-start(), calls=%async_computation.2 | async-start | bytes 1474560 | tf_op jit(solution)/shard_map/all_gather | solution.py:114
  9.4 489.5 %all-reduce.5.cloned.1.call-start = ((), (), s32[]{:S(2)}) async-start(), calls=%async_computation.4 | async-start | bytes 8994816 | tf_op jit(solution)/shard_map/psum | solution.py:160
  13.7 286.7 %copy-start.37 = (f32[1461]{0:T(1024)}, f32[1461]{0:T(1024)S(1)}, u32[]{:S(2)}) copy-start(f32[1461]{0:T(1024)S(1)} %convert_element_type.84) | copy-start | bytes 17536
  22.9 277.5 %copy-start.3 = (bf16[1461,768]{1,0:T(8,128)(2,1)}, bf16[1461,768]{1,0:T(8,128)(2,1)S(1)}, u32[]{:S(2)}) copy-start(bf16[1461,768]{1,0:T(8,128)(2,1)S(1)} %gather_fusion) | copy-start | bytes 6732292
  25.8 299.5 %copy-start.39 = (f32[1461]{0:T(1024)}, f32[1461]{0:T(1024)S(1)}, u32[]{:S(2)}) copy-start(f32[1461]{0:T(1024)S(1)} %add_divide_fusion) | copy-start | bytes 17536
  25.8 64.7 %copy-start.43 = (f32[1461]{0:T(1024)}, f32[1461]{0:T(1024)S(1)}, u32[]{:S(2)}) copy-start(f32[1461]{0:T(1024)S(1)} %broadcast_multiply_fusion.6) | copy-start | bytes 17536
  26.7 63.9 %copy-start.51 = (f32[1461]{0:T(1024)}, f32[1461]{0:T(1024)S(1)}, u32[]{:S(2)}) copy-start(f32[1461]{0:T(1024)S(1)} %add_rsqrt_fusion.1) | copy-start | bytes 17536
  26.7 63.9 %copy-start.55 = (f32[768]{0:T(1024)}, f32[768]{0:T(1024)S(1)}, u32[]{:S(2)}) copy-start(f32[768]{0:T(1024)S(1)} %get-tuple-element.99) | copy-start | bytes 9220
  26.7 63.9 %copy-start.67 = (f32[768]{0:T(1024)}, f32[768]{0:T(1024)S(1)}, u32[]{:S(2)}) copy-start(f32[768]{0:T(1024)S(1)} %get-tuple-element.51) | copy-start | bytes 9220
  310.2 15.1 %copy-start.8 = (f32[1461,768]{1,0:T(8,128)}, f32[1461,768]{1,0:T(8,128)S(1)}, u32[]{:S(2)}) copy-start(f32[1461,768]{1,0:T(8,128)S(1)} %get-tuple-element.69) | copy-start | bytes 13464580
  310.8 14.5 %copy-start.32 = (f32[1461]{0:T(1024)}, f32[1461]{0:T(1024)S(1)}, u32[]{:S(2)}) copy-start(f32[1461]{0:T(1024)S(1)} %add_rsqrt_fusion) | copy-start | bytes 17536
  335.1 267.7 %reduce-scatter.4.cloned.1.call-start = ((), (), s32[]{:S(2)}) async-start(), calls=%async_computation.5 | async-start | bytes 2949120
  351.2 147.7 %copy-start.28 = (f32[1461]{0:T(1024)S(1)}, f32[1461]{0:T(1024)}, u32[]{:S(2)}) copy-start(f32[1461]{0:T(1024)} %copy-done.27) | copy-start | bytes 17536
  351.2 147.7 %copy-start.33 = (f32[1461]{0:T(1024)S(1)}, f32[1461]{0:T(1024)}, u32[]{:S(2)}) copy-start(f32[1461]{0:T(1024)} %copy-done.32) | copy-start | bytes 17536
  357.4 147.3 %copy-start.41 = (f32[1461]{0:T(1024)S(1)}, f32[1461]{0:T(1024)}, u32[]{:S(2)}) copy-start(f32[1461]{0:T(1024)} %copy-done.39) | copy-start | bytes 17536
  357.4 395.6 %all-reduce.7.cloned.1.call-start = ((), (), s32[]{:S(2)}) async-start(), calls=%async_computation.6 | async-start | bytes 14155776 | tf_op jit(solution)/shard_map/psum | solution.py:220
  541.0 15.9 %copy-start.18 = (bf16[6,99,12,1,64]{1,4,2,0,3:T(8,128)(2,1)S(1)}, bf16[6,99,12,1,64]{1,4,2,0,3:T(8,128)(2,1)}, u32[]{:S(2)}) copy-start(bf16[6,99,12,1,64]{1,4,2,0,3:T(8,128)(2,1)} %fusion.83) | copy-start | bytes 2737156
  541.0 15.9 %copy-start.19 = (bf16[6,99,12,1,64]{1,4,2,0,3:T(8,128)(2,1)S(1)}, bf16[6,99,12,1,64]{1,4,2,0,3:T(8,128)(2,1)}, u32[]{:S(2)}) copy-start(bf16[6,99,12,1,64]{1,4,2,0,3:T(8,128)(2,1)} %fusion.82) | copy-start | bytes 2737156
  541.0 15.9 %copy-start.20 = (bf16[6,99,12,1,64]{1,4,2,0,3:T(8,128)(2,1)S(1)}, bf16[6,99,12,1,64]{1,4,2,0,3:T(8,128)(2,1)}, u32[]{:S(2)}) copy-start(bf16[6,99,12,1,64]{1,4,2,0,3:T(8,128)(2,1)} %fusion.81) | copy-start | bytes 2737156
  643.3 29.2 %copy-start.50 = (f32[1461]{0:T(1024)S(1)}, f32[1461]{0:T(1024)}, u32[]{:S(2)}) copy-start(f32[1461]{0:T(1024)} %copy-done.49) | copy-start | bytes 17536
  643.3 29.2 %copy-start.53 = (f32[1461]{0:T(1024)S(1)}, f32[1461]{0:T(1024)}, u32[]{:S(2)}) copy-start(f32[1461]{0:T(1024)} %get-tuple-element.45) | copy-start | bytes 17536
  (54 other events, 292.3 us)
Sparse Core Ops, SparseCore 0:
  9.6 72.6 all-gather.3
  83.9 71.7 all-gather.7
  157.3 29.0 all-gather.5
  335.2 163.6 all-reduce.4
  501.7 47.0 reduce-scatter.3
  640.4 112.5 all-reduce.6
where the time goes:
time: 780 us; the launch traced here: 768 us
  local copies, waits for them, and re-layouts  253 us (32%)
  waiting for transfers between devices  212 us (27%)
  matrix products  148 us (19%)
  other arithmetic  108 us (14%)
  blocking collectives  32.1 us (4%)
  between operations  15.3 us (2%)
    psum x1, waiting for transfers between devices, local(): grad_normed_two, gate_sum = lax.psum((norm_two_part, gate_part), 'mlp')  141 us
    unnamed x157, local copies, waits for them, and re-layouts  76.7 us
    all_gather x1, waiting for transfers between devices, local(): lax.all_gather(w_qkv, 'mlp', axis=1, tiled=True)  55.6 us
    slice x2, local copies, waits for them, and re-layouts, split_heads(): return (shaped[:, :, :, 0, :], shaped[:, :, :, 1, :], shaped[:, :, :, 2, :])  40.2 us
    reshape x2, local copies, waits for them, and re-layouts, split_heads(): shaped = projected.reshape(images, length, head_count, 3, HD)  34.3 us
    psum x1, blocking collectives, local(): lax.psum((d_qkv, d_qkv_bias, d_out, d_out_bias, d_gain_one, d_shift_one,...  23.6 us
    scatter-add x1, other arithmetic, local(): input_grad = full_cot.at[picked].add(grad_rows).astype(LOWER)  22.3 us
    reshape x2, local copies, waits for them, and re-layouts, attend_backward(): return stacked.reshape(images * length, head_count * 3 * HD)  21 us
  transfers between devices with their start and end apart: 6, of which 3 were waited for; matrix products, arithmetic and copies ran while one was open for 56% of the time, Pallas kernels for 0%

commit v1 on v0

v1 whole, which is shorter than its diff:
```python
import functools

import jax
import jax.numpy as jnp
from jax import lax
from jax.experimental import pallas as pl
from jax.experimental.pallas import tpu as pltpu
from jax.sharding import PartitionSpec as P

HD = 64
IMG_DEV = 6
L_MOST = 3
HALF_S = 99
HALF_L = 289

CHUNK = 304
CHUNKS = 1 + L_MOST
PACKED = CHUNK * CHUNKS
SHARE = 8

EPSILON = 1e-06
LOWER = jnp.bfloat16
FLOAT = jnp.float32
MASKED = -1e30
VMEM_LIMIT = 56 * 1024 * 1024


def nn(a, b):
    return lax.dot_general(a, b, (((1,), (0,)), ((), ())), preferred_element_type=FLOAT)


def nt(a, b):
    return lax.dot_general(a, b, (((1,), (1,)), ((), ())), preferred_element_type=FLOAT)


def tn(a, b):
    return lax.dot_general(a, b, (((0,), (0,)), ((), ())), preferred_element_type=FLOAT)


def params(**kwargs):
    return pltpu.CompilerParams(vmem_limit_bytes=VMEM_LIMIT, **kwargs)


def cost(flops, bytes_accessed, transcendentals=0):
    return pl.CostEstimate(
        flops=flops, bytes_accessed=bytes_accessed, transcendentals=transcendentals
    )


def whole(shape, single=True):
    zeros = (0,) * len(shape)
    if single:
        return pl.BlockSpec(shape, lambda *_: zeros, pipeline_mode=pl.Buffered(1))
    return pl.BlockSpec(shape, lambda *_: zeros)


def rows_spec(width, height=CHUNK):
    return pl.BlockSpec((height, width), lambda c: (c, 0))


def norm_stats(values):
    average = jnp.mean(values, axis=-1, keepdims=True)
    centred = values - average
    variance = jnp.mean(centred * centred, axis=-1, keepdims=True)
    inverse = lax.rsqrt(variance + EPSILON)
    return centred * inverse, inverse


def pick_kernel(patches_ref, idx_ref, gains_ref, shifts_ref, router_ref, x_ref, n_ref, gate_ref):
    rows = patches_ref.shape[0]
    places = lax.broadcasted_iota(jnp.int32, (CHUNK, rows), 1)
    onehot = (places == idx_ref[...]).astype(FLOAT).astype(LOWER)
    x = nn(onehot, patches_ref[...])
    x_ref[...] = x.astype(LOWER)
    scaled, _ = norm_stats(x)
    n_ref[...] = (scaled * gains_ref[0:1, :] + shifts_ref[0:1, :]).astype(LOWER)
    logit = jnp.sum(x * router_ref[...], axis=-1, keepdims=True)
    gate_ref[...] = jax.nn.sigmoid(logit)


def pick_rows(patches, idx_col, gains, shifts, router):
    rows, width = patches.shape
    return pl.pallas_call(
        pick_kernel,
        grid=(CHUNKS,),
        in_specs=[
            whole((rows, width)),
            rows_spec(1),
            whole((2, width)),
            whole((2, width)),
            whole((1, width)),
        ],
        out_specs=[rows_spec(width), rows_spec(width), rows_spec(1)],
        out_shape=[
            jax.ShapeDtypeStruct((PACKED, width), LOWER),
            jax.ShapeDtypeStruct((PACKED, width), LOWER),
            jax.ShapeDtypeStruct((PACKED, 1), FLOAT),
        ],
        compiler_params=params(),
        cost_estimate=cost(2 * PACKED * rows * width, 4 * rows * width),
        name="pick_rows",
    )(patches, idx_col, gains, shifts, router)


def pick_cot_kernel(cot_ref, idx_ref, gate_ref, cot_rows_ref, gated_ref):
    rows = cot_ref.shape[1]
    places = lax.broadcasted_iota(jnp.int32, (CHUNK, rows), 1)
    onehot = (places == idx_ref[...]).astype(FLOAT).astype(LOWER)
    cot_rows = nt(onehot, cot_ref[...])
    cot_rows_ref[...] = cot_rows.astype(LOWER)
    gated_ref[...] = (gate_ref[...] * cot_rows).astype(LOWER)


def pick_cot(cot_t, idx_col, gate):
    width, rows = cot_t.shape
    return pl.pallas_call(
        pick_cot_kernel,
        grid=(CHUNKS,),
        in_specs=[whole((width, rows)), rows_spec(1), rows_spec(1)],
        out_specs=[rows_spec(width), rows_spec(width)],
        out_shape=[jax.ShapeDtypeStruct((PACKED, width), LOWER)] * 2,
        compiler_params=params(),
        cost_estimate=cost(2 * PACKED * rows * width, 4 * rows * width),
        name="pick_cot",
    )(cot_t, idx_col, gate)


def load_attention(gathered_ref, weights):
    part = gathered_ref.shape[2]
    per_kind = SHARE // 4
    places = gathered_ref.shape[1]
    for kind in range(4):
        for place in range(places):
            for piece in range(per_kind):
                start = ((kind * places + place) * per_kind + piece) * part
                weights[start : start + part, :] = gathered_ref[kind * per_kind + piece, place]


def pair_mask(head):
    lanes = lax.broadcasted_iota(jnp.int32, (1, 2 * HD), 1)
    return (lanes < HD) if head % 2 == 0 else (lanes >= HD)


def keep_head(values, head):
    return jnp.where(pair_mask(head), values, jnp.zeros_like(values))


def forward_kernel(
    n_ref,
    x_ref,
    gathered_ref,
    bias_ref,
    seg_col_ref,
    seg_row_ref,
    post_ref,
    gains_ref,
    shifts_ref,
    proj_ref,
    mix_ref,
    lse_ref,
    hidden_ref,
    normed_ref,
    weights,
):
    width = n_ref.shape[1]

    @pl.when(pl.program_id(0) == 0)
    def _():
        load_attention(gathered_ref, weights)

    normed = n_ref[...]
    for kind in range(3):
        cols = slice(kind * width, (kind + 1) * width)
        proj_ref[:, cols] = (nt(normed, weights[cols, :]) + bias_ref[:, cols]).astype(LOWER)
    outside = jnp.where(seg_col_ref[...] == seg_row_ref[0], 0.0, MASKED)
    lse_all = jnp.zeros((CHUNK, 128), FLOAT)
    lanes = lax.broadcasted_iota(jnp.int32, (1, 128), 1)
    for pair in range(width // (2 * HD)):
        cols = slice(pair * 2 * HD, (pair + 1) * 2 * HD)
        q = proj_ref[:, cols] * LOWER(HD**-0.5)
        k = proj_ref[:, width + pair * 2 * HD : width + (pair + 1) * 2 * HD]
        v = proj_ref[:, 2 * width + pair * 2 * HD : 2 * width + (pair + 1) * 2 * HD]
        mixed = None
        for head in (2 * pair, 2 * pair + 1):
            scores = nt(q, keep_head(k, head)) + outside
            largest = jnp.max(scores, axis=-1, keepdims=True)
            powered = jnp.exp(scores - largest)
            total = jnp.sum(powered, axis=-1, keepdims=True)
            probs = (powered * (1.0 / total)).astype(LOWER)
            part = nn(probs, keep_head(v, head))
            mixed = part if mixed is None else mixed + part
            lse_all = jnp.where(lanes == head, largest + jnp.log(total), lse_all)
        mix_ref[:, cols] = mixed.astype(LOWER)
    lse_ref[0] = jnp.transpose(lse_all)[0:16, :]
    attn = nn(mix_ref[...], weights[3 * width :, :]) + post_ref[0:1, :]
    hidden = x_ref[...].astype(FLOAT) + attn
    hidden_ref[...] = hidden
    scaled, _ = norm_stats(hidden)
    normed_ref[...] = (scaled * gains_ref[1:2, :] + shifts_ref[1:2, :]).astype(LOWER)


def forward_attention(normed, x, gathered, bias, seg_col, seg_row, post, gains, shifts):
    width = x.shape[1]
    return pl.pallas_call(
        forward_kernel,
        grid=(CHUNKS,),
        in_specs=[
            rows_spec(width),
            rows_spec(width),
            whole(gathered.shape),
            whole((1, 3 * width)),
            rows_spec(1),
            pl.BlockSpec((1, 1, CHUNK), lambda c: (c, 0, 0)),
            whole((2, width)),
            whole((2, width)),
            whole((2, width)),
        ],
        out_specs=[
            rows_spec(3 * width),
            rows_spec(width),
            pl.BlockSpec((1, 16, CHUNK), lambda c: (c, 0, 0)),
            rows_spec(width),
            rows_spec(width),
        ],
        out_shape=[
            jax.ShapeDtypeStruct((PACKED, 3 * width), LOWER),
            jax.ShapeDtypeStruct((PACKED, width), LOWER),
            jax.ShapeDtypeStruct((CHUNKS, 16, CHUNK), FLOAT),
            jax.ShapeDtypeStruct((PACKED, width), FLOAT),
            jax.ShapeDtypeStruct((PACKED, width), LOWER),
        ],
        scratch_shapes=[pltpu.VMEM((4 * width, width), LOWER)],
        compiler_params=params(),
        cost_estimate=cost(2 * PACKED * width * 8 * width, 20 * PACKED * width),
        name="forward_attention",
    )(normed, x, gathered, bias, seg_col, seg_row, post, gains, shifts)


def gelu_pair(u):
    cdf = 0.5 * (1.0 + lax.erf(u * (0.5**0.5)))
    density = jnp.exp(-0.5 * u * u) * 0.3989422804014327
    return u * cdf, cdf + u * density


def mlp_kernel(
    n_ref,
    gated_ref,
    weights_ref,
    own_down_ref,
    bias_ref,
    act_ref,
    pre_ref,
    grad_ref,
    gate_ref,
    out_ref,
):
    place, chunk = pl.program_id(0), pl.program_id(1)
    width = n_ref.shape[1]
    hidden = bias_ref.shape[2]
    rows = pl.ds(pl.multiple_of(chunk * CHUNK, 16), CHUNK)
    up = weights_ref[:, 0, 0].reshape(width, hidden)
    down = weights_ref[:, 0, 1].reshape(hidden, width)
    normed = n_ref[rows, :]
    gated = gated_ref[rows, :]
    pre_act = nn(normed, up) + bias_ref[0]
    activation, slope = gelu_pair(pre_act)
    activation = activation.astype(LOWER)
    grad_act = nt(gated, down)
    grad_pre = (grad_act * slope).astype(LOWER)
    act_ref[...] = activation
    pre_ref[...] = grad_pre
    grad_part = nt(grad_pre, up)
    gate_part = jnp.sum(activation.astype(FLOAT) * grad_act, axis=-1, keepdims=True)
    out_part = nn(activation, own_down_ref[0])

    @pl.when(place == 0)
    def _():
        grad_ref[rows, :] = grad_part
        gate_ref[rows, :] = gate_part
        out_ref[rows, :] = out_part

    @pl.when(place > 0)
    def _():
        grad_ref[rows, :] += grad_part
        gate_ref[rows, :] += gate_part
        out_ref[rows, :] += out_part


def mlp_both(normed, gated, weights, own_down, bias):
    width = normed.shape[1]
    places, hidden = bias.shape[0], bias.shape[2]
    own = own_down.shape[2]
    share, part = weights.shape[0], weights.shape[3]
    first = lambda j, c: (jnp.where(j == 0, c, CHUNKS), 0)
    return pl.pallas_call(
        mlp_kernel,
        grid=(places, CHUNKS),
        in_specs=[
            whole((PACKED, width)),
            whole((PACKED, width)),
            pl.BlockSpec((share, 1, 2, part, width), lambda j, c: (0, j, 0, 0, 0)),
            pl.BlockSpec((1, hidden, own), lambda j, c: (j, 0, 0)),
            pl.BlockSpec((1, 1, hidden), lambda j, c: (j, 0, 0)),
        ],
        out_specs=[
            pl.BlockSpec((CHUNK, hidden), first),
            pl.BlockSpec((CHUNK, hidden), first),
            whole((PACKED, width), False),
            whole((PACKED, 1), False),
            whole((PACKED, own), False),
        ],
        out_shape=[
            jax.ShapeDtypeStruct((PACKED + CHUNK, hidden), LOWER),
            jax.ShapeDtypeStruct((PACKED + CHUNK, hidden), LOWER),
            jax.ShapeDtypeStruct((PACKED, width), FLOAT),
            jax.ShapeDtypeStruct((PACKED, 1), FLOAT),
            jax.ShapeDtypeStruct((PACKED, own), FLOAT),
        ],
        compiler_params=params(),
        cost_estimate=cost(
            2 * PACKED * places * hidden * (3 * width + own), 4 * places * hidden * width
        ),
        name="mlp_both",
    )(normed, gated, weights, own_down, bias)


def backward_kernel(
    grad_ref,
    gate_part_ref,
    hidden_ref,
    x_ref,
    cot_ref,
    gate_ref,
    proj_ref,
    lse_ref,
    gathered_ref,
    seg_col_ref,
    seg_row_ref,
    post_ref,
    gains_ref,
    gproj_ref,
    ghid_ref,
    glow_ref,
    logit_ref,
    sums_ref,
    weights,
    gmix,
):
    width = x_ref.shape[1]
    chunk = pl.program_id(0)

    @pl.when(chunk == 0)
    def _():
        part = gathered_ref.shape[2]
        per_kind, places = SHARE // 4, gathered_ref.shape[1]
        for place in range(places):
            for piece in range(per_kind):
                start = (place * per_kind + piece) * part
                weights[start : start + part, :] = gathered_ref[3 * per_kind + piece, place]
        sums_ref[...] = jnp.zeros_like(sums_ref)

    hidden = hidden_ref[...]
    scaled, inverse = norm_stats(hidden)
    grad_out = grad_ref[...]
    weighted = grad_out * gains_ref[1:2, :]
    centre_term = jnp.mean(weighted, axis=-1, keepdims=True)
    scale_term = jnp.mean(weighted * scaled, axis=-1, keepdims=True)
    grad_hidden = inverse * (weighted - centre_term - scaled * scale_term)
    gate = gate_ref[...]
    gated = gate * cot_ref[...].astype(FLOAT)
    grad_attn = grad_hidden + gated
    ghid_ref[...] = grad_hidden
    low = grad_attn.astype(LOWER)
    glow_ref[...] = low
    attn = hidden - x_ref[...].astype(FLOAT)
    dotted = jnp.sum(gated * (attn + post_ref[1:2, :]), axis=-1, keepdims=True)
    logit_ref[...] = (1.0 - gate) * (dotted + gate_part_ref[...])
    sums_ref[0:1, :] += jnp.sum(grad_out * scaled, axis=0, keepdims=True)
    sums_ref[1:2, :] += jnp.sum(grad_out, axis=0, keepdims=True)
    sums_ref[2:3, :] += jnp.sum(grad_attn, axis=0, keepdims=True)
    sums_ref[3:4, :] += jnp.sum(gated, axis=0, keepdims=True)
    gmix[...] = nt(low, weights[...]).astype(LOWER)
    outside = jnp.where(seg_col_ref[...] == seg_row_ref[0], 0.0, MASKED)
    for pair in range(width // (2 * HD)):
        cols = slice(pair * 2 * HD, (pair + 1) * 2 * HD)
        k_cols = slice(width + pair * 2 * HD, width + (pair + 1) * 2 * HD)
        v_cols = slice(2 * width + pair * 2 * HD, 2 * width + (pair + 1) * 2 * HD)
        q = proj_ref[:, cols] * LOWER(HD**-0.5)
        k = proj_ref[:, k_cols]
        v = proj_ref[:, v_cols]
        g = gmix[:, cols]
        grad_q, grad_k, grad_v = None, None, None
        for head in (2 * pair, 2 * pair + 1):
            own_k = keep_head(k, head)
            scores = nt(own_k, q) + outside
            probs = jnp.exp(scores - lse_ref[0, head : head + 1, :])
            grad_probs = nt(keep_head(v, head), g)
            inner = jnp.sum(probs * grad_probs, axis=0, keepdims=True)
            grad_scores = (probs * (grad_probs - inner)).astype(LOWER)
            one_v = nn(probs.astype(LOWER), g)
            one_k = nn(grad_scores, q)
            one_q = tn(grad_scores, own_k)
            if head % 2 == 0:
                grad_q, grad_k, grad_v = one_q, one_k, one_v
            else:
                first = pair_mask(0)
                grad_q = grad_q + one_q
                grad_k = jnp.where(first, grad_k, one_k)
                grad_v = jnp.where(first, grad_v, one_v)
        gproj_ref[:, cols] = (grad_q * HD**-0.5).astype(LOWER)
        gproj_ref[:, k_cols] = grad_k.astype(LOWER)
        gproj_ref[:, v_cols] = grad_v.astype(LOWER)


def backward_attention(
    grad, gate_part, hidden, x, cot_rows, gate, proj, lse, gathered, seg_col, seg_row, post, gains
):
    width = x.shape[1]
    return pl.pallas_call(
        backward_kernel,
        grid=(CHUNKS,),
        in_specs=[
            rows_spec(width),
            rows_spec(1),
            rows_spec(width),
            rows_spec(width),
            rows_spec(width),
            rows_spec(1),
            rows_spec(3 * width),
            pl.BlockSpec((1, 16, CHUNK), lambda c: (c, 0, 0)),
            whole(gathered.shape),
            rows_spec(1),
            pl.BlockSpec((1, 1, CHUNK), lambda c: (c, 0, 0)),
            whole((2, width)),
            whole((2, width)),
        ],
        out_specs=[
            rows_spec(3 * width),
            rows_spec(width),
            rows_spec(width),
            rows_spec(1),
            whole((8, width), False),
        ],
        out_shape=[
            jax.ShapeDtypeStruct((PACKED, 3 * width), LOWER),
            jax.ShapeDtypeStruct((PACKED, width), FLOAT),
            jax.ShapeDtypeStruct((PACKED, width), LOWER),
            jax.ShapeDtypeStruct((PACKED, 1), FLOAT),
            jax.ShapeDtypeStruct((8, width), FLOAT),
        ],
        scratch_shapes=[pltpu.VMEM((width, width), LOWER), pltpu.VMEM((CHUNK, width), LOWER)],
        compiler_params=params(),
        cost_estimate=cost(2 * PACKED * width * 14 * width, 20 * PACKED * width),
        name="backward_attention",
    )(grad, gate_part, hidden, x, cot_rows, gate, proj, lse, gathered, seg_col, seg_row, post, gains)


def first_norm_kernel(
    gproj_ref,
    gathered_ref,
    x_ref,
    ghid_ref,
    logit_ref,
    gains_ref,
    router_ref,
    rows_ref,
    sums_ref,
    weights,
):
    width = x_ref.shape[1]

    @pl.when(pl.program_id(0) == 0)
    def _():
        part = gathered_ref.shape[2]
        per_kind, places = SHARE // 4, gathered_ref.shape[1]
        for kind in range(3):
            for place in range(places):
                for piece in range(per_kind):
                    start = ((kind * places + place) * per_kind + piece) * part
                    weights[start : start + part, :] = gathered_ref[kind * per_kind + piece, place]
        sums_ref[...] = jnp.zeros_like(sums_ref)

    grad_out = nn(gproj_ref[...], weights[...])
    x = x_ref[...].astype(FLOAT)
    scaled, inverse = norm_stats(x)
    weighted = grad_out * gains_ref[0:1, :]
    centre_term = jnp.mean(weighted, axis=-1, keepdims=True)
    scale_term = jnp.mean(weighted * scaled, axis=-1, keepdims=True)
    grad_norm = inverse * (weighted - centre_term - scaled * scale_term)
    logit = logit_ref[...]
    rows_ref[...] = (ghid_ref[...] + grad_norm + logit * router_ref[...]).astype(LOWER)
    sums_ref[0:1, :] += jnp.sum(grad_out * scaled, axis=0, keepdims=True)
    sums_ref[1:2, :] += jnp.sum(grad_out, axis=0, keepdims=True)
    sums_ref[2:3, :] += jnp.sum(logit * x, axis=0, keepdims=True)


def first_norm(gproj, gathered, x, ghid, logit, gains, router):
    width = x.shape[1]
    return pl.pallas_call(
        first_norm_kernel,
        grid=(CHUNKS,),
        in_specs=[
            rows_spec(3 * width),
            whole(gathered.shape),
            rows_spec(width),
            rows_spec(width),
            rows_spec(1),
            whole((2, width)),
            whole((1, width)),
        ],
        out_specs=[rows_spec(width), whole((8, width), False)],
        out_shape=[
            jax.ShapeDtypeStruct((PACKED, width), LOWER),
            jax.ShapeDtypeStruct((8, width), FLOAT),
        ],
        scratch_shapes=[pltpu.VMEM((3 * width, width), LOWER)],
        compiler_params=params(),
        cost_estimate=cost(2 * PACKED * width * 3 * width, 16 * PACKED * width),
        name="first_norm",
    )(gproj, gathered, x, ghid, logit, gains, router)


def scatter_kernel(cot_ref, idx_ref, rows_ref, out_ref):
    block = out_ref.shape[0]
    places = lax.broadcasted_iota(jnp.int32, (block, PACKED), 0) + pl.program_id(0) * block
    onehot = (places == idx_ref[...]).astype(FLOAT).astype(LOWER)
    out_ref[...] = (cot_ref[...].astype(FLOAT) + nn(onehot, rows_ref[...])).astype(LOWER)


def scatter_rows(cot, idx_row, rows):
    total, width = cot.shape
    block = 400
    return pl.pallas_call(
        scatter_kernel,
        grid=(pl.cdiv(total, block),),
        in_specs=[
            rows_spec(width, block),
            whole((1, PACKED)),
            whole((PACKED, width)),
        ],
        out_specs=rows_spec(width, block),
        out_shape=jax.ShapeDtypeStruct((total, width), LOWER),
        compiler_params=params(),
        cost_estimate=cost(2 * PACKED * total * width, 4 * total * width),
        name="scatter_rows",
    )(cot, idx_row, rows)


def block_out_kernel(patch_ref, idx_ref, branch_ref, out_ref):
    total = out_ref.shape[1]
    places = lax.broadcasted_iota(jnp.int32, (PACKED, total), 1)
    onehot = (places == idx_ref[...]).astype(FLOAT).astype(LOWER)
    added = nn(branch_ref[...], onehot)
    out_ref[...] = (patch_ref[...].astype(FLOAT) + added).astype(LOWER)


def block_out_rows(patch_t, idx_col, branch_t):
    own, total = patch_t.shape
    return pl.pallas_call(
        block_out_kernel,
        out_shape=jax.ShapeDtypeStruct((own, total), LOWER),
        compiler_params=params(),
        cost_estimate=cost(2 * PACKED * total * own, 4 * total * own),
        name="block_out_rows",
    )(patch_t, idx_col, branch_t)


def share_groups(rows):
    return [list(range(first, first + SHARE)) for first in range(0, rows, SHARE)]


def ring(value, axis, size):
    got = [value]
    step = [(i, (i + 1) % size) for i in range(size)]
    for _ in range(size - 1):
        got.append(lax.ppermute(got[-1], axis, step))
    return got


def turned(values, place):
    size = values.shape[0]
    back = jnp.concatenate([values[:1], values[:0:-1]], axis=0)
    twice = jnp.concatenate([back, back], axis=0)
    return lax.dynamic_slice_in_dim(twice, (size - place) % size, size, 0)


def pack_slots(picked, live_slots):
    small = IMG_DEV * HALF_S
    named = jnp.where(live_slots == 1, picked, -1)

    def padded(parts, fill):
        have = sum(p.shape[0] for p in parts)
        return jnp.concatenate([*parts, jnp.full((CHUNK - have,), fill, jnp.int32)])

    always = IMG_DEV - L_MOST
    idx = [padded([named[: always * HALF_S]], -1)]
    seg = [padded([jnp.repeat(jnp.arange(always, dtype=jnp.int32), HALF_S)], always)]
    for j in range(L_MOST):
        first = small + j * HALF_L
        alive = live_slots[first] == 1
        other = IMG_DEV - 1 - j
        large_idx = padded([named[first : first + HALF_L]], -1)
        small_idx = padded([named[other * HALF_S : (other + 1) * HALF_S]], -1)
        idx.append(jnp.where(alive, large_idx, small_idx))
        length = jnp.where(alive, HALF_L, HALF_S)
        seg.append((jnp.arange(CHUNK, dtype=jnp.int32) >= length).astype(jnp.int32))
    return jnp.concatenate(idx), jnp.concatenate(seg)


def local(
    rows_size,
    mlp_size,
    patches,
    w_qkv,
    qkv_bias,
    w_out,
    post_bias,
    w_up,
    up_bias,
    w_down,
    norm_gains,
    norm_shifts,
    router,
    picked,
    live_slots,
    cotangent,
):
    width = patches.shape[1]
    mlp_index = lax.axis_index("mlp")
    share_index = lax.axis_index("rows") % SHARE
    groups = share_groups(rows_size)
    own = w_out.shape[0]
    heads_here = own // HD
    router_row = router.reshape(1, width)

    attn_shard = jnp.concatenate(
        [
            w_qkv.T.reshape(heads_here, 3, HD, width).transpose(1, 0, 2, 3).reshape(3 * own, width),
            w_out,
        ],
        axis=0,
    )
    part = attn_shard.shape[0] // SHARE
    attn_piece = lax.dynamic_slice_in_dim(attn_shard, share_index * part, part, 0)
    attn_parts = jnp.stack(ring(attn_piece, "mlp", mlp_size), axis=0)
    attn_all = lax.all_gather(attn_parts, "rows", axis_index_groups=groups, axis=0)
    mlp_part = w_up.shape[0] // SHARE
    mlp_piece = jnp.stack(
        [
            lax.dynamic_slice_in_dim(w_up, share_index * mlp_part, mlp_part, 0),
            lax.dynamic_slice_in_dim(w_down, share_index * mlp_part, mlp_part, 0),
        ],
        axis=0,
    )
    mlp_parts = jnp.stack(ring(mlp_piece, "mlp", mlp_size), axis=0)
    mlp_all = lax.all_gather(mlp_parts, "rows", axis_index_groups=groups, axis=0)
    cot_t = lax.all_gather(cotangent.T, "mlp", axis=0, tiled=True)
    up_bias_all = turned(lax.all_gather(up_bias, "mlp", axis=0), mlp_index)[:, None, :]
    kinds = jnp.stack([qkv_bias[0], jnp.zeros_like(qkv_bias[0]), qkv_bias[1]])
    bias = turned(kinds.reshape(3, mlp_size, own).transpose(1, 0, 2), mlp_index)
    bias = bias.transpose(1, 0, 2).reshape(1, 3 * width)

    idx, seg = pack_slots(picked, live_slots)
    idx_col, idx_row = idx.reshape(PACKED, 1), idx.reshape(1, PACKED)
    seg_col, seg_row = seg.reshape(PACKED, 1), seg.reshape(CHUNKS, 1, CHUNK)

    x, normed_one, gate = pick_rows(patches, idx_col, norm_gains, norm_shifts, router_row)
    proj, mix, lse, hidden, normed_two = forward_attention(
        normed_one, x, attn_all, bias, seg_col, seg_row, post_bias, norm_gains, norm_shifts
    )
    cot_rows, gated = pick_cot(cot_t, idx_col, gate)

    feature_start = mlp_index * own
    down_all = mlp_all[:, :, 1].transpose(1, 0, 2, 3).reshape(mlp_size, w_down.shape[0], width)
    own_down = lax.dynamic_slice_in_dim(down_all, feature_start, own, 2)
    act, grad_pre, grad_two, gate_part, mlp_own = mlp_both(
        normed_two, gated, mlp_all, own_down, up_bias_all
    )
    act, grad_pre = act[:PACKED], grad_pre[:PACKED]
    d_down = tn(act, gated).astype(LOWER)
    d_up = tn(normed_two, grad_pre).astype(LOWER)
    d_up_bias = jnp.sum(grad_pre.astype(FLOAT), axis=0)

    attn_own = lax.dynamic_slice_in_dim(hidden - x.astype(FLOAT), feature_start, own, 1)
    bias_own = lax.dynamic_slice_in_dim(post_bias[1], feature_start, own, 0)
    branch = gate * (attn_own + mlp_own + bias_own)
    patch_t = lax.dynamic_slice_in_dim(patches, feature_start, own, 1).T
    block_out = block_out_rows(patch_t, idx_col, branch.astype(LOWER).T).T

    grad_proj, grad_hidden, grad_low, logit, sums_two = backward_attention(
        grad_two,
        gate_part,
        hidden,
        x,
        cot_rows,
        gate,
        proj,
        lse,
        attn_all,
        seg_col,
        seg_row,
        post_bias,
        norm_gains,
    )
    d_out = tn(mix[:, :own], grad_low).astype(LOWER)
    own_proj = jnp.concatenate(
        [grad_proj[:, kind * width : kind * width + own] for kind in range(3)], axis=1
    )
    d_qkv_t = tn(own_proj, normed_one).astype(LOWER)
    bias_grad = jnp.sum(own_proj.astype(FLOAT), axis=0)
    rows_grad, sums_one = first_norm(
        grad_proj, attn_all, x, grad_hidden, logit, norm_gains, router_row
    )
    input_grad = scatter_rows(cot_t.T, idx_row, rows_grad)

    d_down, d_up, d_out, d_qkv_t = lax.psum((d_down, d_up, d_out, d_qkv_t), "rows")
    small = jnp.concatenate(
        [
            sums_two[:4],
            sums_one[:3],
            d_up_bias.reshape(1, width),
            jnp.pad(bias_grad, (0, width - 3 * own)).reshape(1, width),
        ],
        axis=0,
    )
    small = lax.psum(small, "rows")
    d_qkv = (
        d_qkv_t.astype(FLOAT)
        .reshape(3, heads_here, HD, width)
        .transpose(1, 0, 2, 3)
        .reshape(3 * own, width)
        .T
    )
    d_qkv_bias = jnp.stack([small[8, :own], small[8, 2 * own : 3 * own]])
    return (
        block_out,
        input_grad,
        d_qkv,
        d_qkv_bias,
        d_out.astype(FLOAT),
        small[2:4],
        d_up.astype(FLOAT),
        small[7],
        d_down.astype(FLOAT),
        jnp.stack([small[4], small[0]]),
        jnp.stack([small[5], small[1]]),
        small[6],
    )


def solution(mesh):
    in_specs = (
        P("rows", None),
        P(None, "mlp"),
        P(),
        P("mlp", None),
        P(),
        P(None, "mlp"),
        P("mlp"),
        P("mlp", None),
        P(),
        P(),
        P(),
        P("rows"),
        P("rows"),
        P("rows", "mlp"),
    )
    out_specs = (
        P("rows", "mlp"),
        P("rows", None),
        P(None, "mlp"),
        P(None, "mlp"),
        P("mlp", None),
        P(),
        P(None, "mlp"),
        P("mlp"),
        P("mlp", None),
        P(),
        P(),
        P(),
    )
    body = functools.partial(local, mesh.shape["rows"], mesh.shape["mlp"])
    return jax.shard_map(body, mesh=mesh, in_specs=in_specs, out_specs=out_specs, check_vma=False)
```

time: 780 us -> 425 us (0.54); the launches traced: 768 us -> 424 us
  local copies, waits for them, and re-layouts: 253 us -> 38.4 us
  Pallas kernels: 0 us -> 136 us
  matrix products: 148 us -> 12.4 us
  other arithmetic: 108 us -> 17.9 us
  waiting for transfers between devices: 212 us -> 151 us
  blocking collectives: 32.1 us -> 42.8 us
  starting transfers between devices: 0.24 us -> 9.17 us
    pallas_call x0 -> x8, Pallas kernels: none -> 136 us  [the longest x1 34.6 us: backward_attention(): pl.pallas_call(backward_kernel, grid=(CHUNKS,), in_specs=[rows_spec(width...]
    dot_general x26 -> x4, matrix products: 148 us -> 12.4 us  [tn(): lax.dot_general(a, b, (((0,), (0,)), ((), ())), preferred_element_type=FL...]
    psum x2 -> x1, waiting for transfers between devices: 154 us -> 56.7 us  [local(): lax.psum((d_down, d_up, d_out, d_qkv_t), 'rows')]
    ppermute x0 -> x6, waiting for transfers between devices: none -> 76.4 us  [ring(): got.append(lax.ppermute(got[-1], axis, step))]
    reshape x13 -> x11, local copies, waits for them, and re-layouts: 80.7 us -> 6.08 us  [the longest x2 1.74 us: local(): seg_col, seg_row = (seg.reshape(PACKED, 1), seg.reshape(CHUNKS, 1, CHUNK))]
    unnamed x157 -> x36, local copies, waits for them, and re-layouts: 76.7 us -> 4.1 us
    slice x10 -> x16, local copies, waits for them, and re-layouts: 47.3 us -> 4.32 us  [the longest x1 1.59 us: local(): grad_proj[:, kind * width:kind * width + own]]
    all_gather x3, waiting for transfers between devices: 55.6 us -> 17.3 us  [the longest x1 17.3 us: local(): lax.all_gather(mlp_parts, 'rows', axis_index_groups=groups, axis=0)]
  transfers between devices with their start and end apart: 6 -> 10, of which waited for: 3 -> 8; matrix products, arithmetic and copies ran while one was open for 56% -> 9% of each run, Pallas kernels for 0% -> 14%
where the time goes in v1:
time: 425 us; the launch traced here: 424 us
  waiting for transfers between devices  151 us (36%)
  Pallas kernels  136 us (32%)
  blocking collectives  42.8 us (10%)
  local copies, waits for them, and re-layouts  38.4 us (9%)
  other arithmetic  17.9 us (4%)
  between operations  16.1 us (4%)
  matrix products  12.4 us (3%)
  starting transfers between devices  9.17 us (2%)
    ppermute x6, waiting for transfers between devices, ring(): got.append(lax.ppermute(got[-1], axis, step))  76.4 us
    psum x1, waiting for transfers between devices, local(): lax.psum((d_down, d_up, d_out, d_qkv_t), 'rows')  56.7 us
    pallas_call x1, Pallas kernels, backward_attention(): pl.pallas_call(backward_kernel, grid=(CHUNKS,), in_specs=[rows_spec(width...  34.6 us
    pallas_call x1, Pallas kernels, mlp_both(): pl.pallas_call(mlp_kernel, grid=(places, CHUNKS), in_specs=[whole((PACKED...  32.6 us
    pallas_call x1, Pallas kernels, forward_attention(): pl.pallas_call(forward_kernel, grid=(CHUNKS,), in_specs=[rows_spec(width)...  25.6 us
    psum x1, blocking collectives, local(): small = lax.psum(small, 'rows')  23.9 us
    all_gather x1, blocking collectives, local(): lax.all_gather(up_bias, 'mlp', axis=0)  18.9 us
    all_gather x1, waiting for transfers between devices, local(): lax.all_gather(mlp_parts, 'rows', axis_index_groups=groups, axis=0)  17.3 us
  transfers between devices with their start and end apart: 10, of which 8 were waited for; matrix products, arithmetic and copies ran while one was open for 9% of the time, Pallas kernels for 14%

profile of v1, /device:TPU:0, one launch (start us, length us, event | category | flops | bytes accessed | tf_op | source)
XLA Modules:
  0.0 424.1 jit_solution(16000074564453360503)
XLA Ops:
  9.3 3.1 collective-permute-start
  12.4 5.9 %collective-permute-done = bf16[96,768]{1,0:T(8,128)(2,1)S(1)} collective-permute-done((bf16[96,768]{1,0:T(8,128)(2,1)S(1)}, bf16[96,768]{1,0:T(8,128)(2,1)S(1)}, u32[]{:S(2)}, u32[]{:S(2)}) %collective-permute-start) | collective-permute-done | bytes 147488 | tf_op jit(solution)/shard_map/ppermute | solution.py:576
  18.3 7.2 %collective-permute-done.1 = bf16[96,768]{1,0:T(8,128)(2,1)S(1)} collective-permute-done((bf16[96,768]{1,0:T(8,128)(2,1)S(1)}, bf16[96,768]{1,0:T(8,128)(2,1)S(1)}, u32[]{:S(2)}, u32[]{:S(2)}) %collective-permute-start.1) | collective-permute-done | bytes 147488 | tf_op jit(solution)/shard_map/ppermute | solution.py:576
  25.5 10.7 %collective-permute-done.2 = bf16[96,768]{1,0:T(8,128)(2,1)S(1)} collective-permute-done((bf16[96,768]{1,0:T(8,128)(2,1)S(1)}, bf16[96,768]{1,0:T(8,128)(2,1)S(1)}, u32[]{:S(2)}, u32[]{:S(2)}) %collective-permute-start.2) | collective-permute-done | bytes 147488 | tf_op jit(solution)/shard_map/ppermute | solution.py:576
  38.2 16.6 %collective-permute-done.3 = bf16[2,96,768]{2,1,0:T(8,128)(2,1)S(1)} collective-permute-done((bf16[2,96,768]{2,1,0:T(8,128)(2,1)S(1)}, bf16[2,96,768]{2,1,0:T(8,128)(2,1)S(1)}, u32[]{:S(2)}, u32[]{:S(2)}) %collective-permute-start.3) | collective-permute-done | bytes 294944 | tf_op jit(solution)/shard_map/ppermute | solution.py:576
  57.2 18.0 %collective-permute-done.4 = bf16[2,96,768]{2,1,0:T(8,128)(2,1)S(1)} collective-permute-done((bf16[2,96,768]{2,1,0:T(8,128)(2,1)S(1)}, bf16[2,96,768]{2,1,0:T(8,128)(2,1)S(1)}, u32[]{:S(2)}, u32[]{:S(2)}) %collective-permute-start.4) | collective-permute-done | bytes 294944 | tf_op jit(solution)/shard_map/ppermute | solution.py:576
  75.2 3.6 collective-permute-start.5
  78.8 18.0 %collective-permute-done.5 = bf16[2,96,768]{2,1,0:T(8,128)(2,1)S(1)} collective-permute-done((bf16[2,96,768]{2,1,0:T(8,128)(2,1)S(1)}, bf16[2,96,768]{2,1,0:T(8,128)(2,1)S(1)}, u32[]{:S(2)}, u32[]{:S(2)}) %collective-permute-start.5) | collective-permute-done | bytes 294944 | tf_op jit(solution)/shard_map/ppermute | solution.py:576
  106.2 18.9 %all-gather.3 = f32[4,1,768]{2,1,0:T(1,128)S(1)} all-gather(f32[1,1,768]{2,1,0:T(1,128)S(1)} %reshape.99), channel_id=4, replica_groups=mesh['rows'=8,'mlp'=4] {'mlp'}, dimensions={0}, use_global_device_ids=true | all-gather | bytes 15360 | tf_op jit(solution)/shard_map/all_gather | solution.py:658
  125.9 9.8 %pick_rows.1 = (bf16[1216,768]{1,0:T(8,128)(2,1)}, bf16[1216,768]{1,0:T(8,128)(2,1)}, f32[1216,1]{1,0:T(8,128)}) custom-call(bf16[2322,768]{1,0:T(8,128)(2,1)} %patches_ref.1, s32[1216,1]{1,0:T(8,128)} %reshape.105.idx_ref, f32[2,768]{1,0:T(2,128)} %gains_ref.7, f32[2,768]{1,0:T(2,128)} %shifts_ref.3, f32[1,768]{1,0:T(1,128)} %reshape.80.router_ref), custom_call_target="tpu_custom_call" | custom-call | flops 4336975872 | bytes 7133184 | tf_op jit(solution)/shard_map/pick_rows/pallas_call | solution.py:83
  135.7 3.7 convert_element_type.48
  145.7 6.0 %copy.72 = bf16[768,2322]{0,1:T(8,128)(2,1)} copy(bf16[768,2322]{1,0:T(8,128)(2,1)} %all-gather.8.cloned.1.call-done.cot_ref) | data formatting | bytes 7133184 | tf_op jit(solution)/shard_map/all_gather | solution.py:657
  151.7 8.9 %pick_cot.1 = (bf16[1216,768]{1,0:T(8,128)(2,1)}, bf16[1216,768]{1,0:T(8,128)(2,1)}) custom-call(bf16[768,2322]{1,0:T(8,128)(2,1)} %all-gather.8.cloned.1.call-done.cot_ref, s32[1216,1]{1,0:T(8,128)} %reshape.105.idx_ref, f32[1216,1]{1,0:T(8,128)} %get-tuple-element.34.gate_ref), custom_call_target="tpu_custom_call" | custom-call | flops 4336975872 | bytes 7133184 | tf_op jit(solution)/shard_map/pick_cot/pallas_call | solution.py:116
  160.6 25.6 %forward_attention.1 = (bf16[1216,2304]{1,0:T(8,128)(2,1)}, bf16[1216,768]{1,0:T(8,128)(2,1)}, f32[4,16,304]{2,1,0:T(8,128)}, f32[1216,768]{1,0:T(8,128)}, bf16[1216,768]{1,0:T(8,128)(2,1)}) custom-call(bf16[1216,768]{1,0:T(8,128)(2,1)} %get-tuple-element.35.n_ref, bf16[1216,768]{1,0:T(8,128)(2,1)} %get-tuple-element.36.x_ref, ...), custom_call_target="tpu_custom_call" | custom-call | flops 11475615744 | bytes 18677760 | tf_op jit(solution)/shard_map/forward_attention/pallas_call | solution.py:204
  186.2 5.4 %copy.66 = f32[1216,768]{0,1:T(8,128)} copy(f32[1216,768]{1,0:T(8,128)} %get-tuple-element.37.hidden_ref) | data formatting | bytes 7471104 | tf_op jit(solution)/shard_map/forward_attention/pallas_call | solution.py:204
  191.6 17.3 %all-gather.12.cloned.1.call-done = bf16[32,2,96,768]{3,2,1,0:T(8,128)(2,1)} async-done(((bf16[4,2,96,768]{3,2,1,0:T(8,128)(2,1)}), bf16[32,2,96,768]{3,2,1,0:T(8,128)(2,1)}) %all-gather.12.cloned.1.call-update) | async-done | bytes 9437200 | tf_op jit(solution)/shard_map/all_gather | solution.py:656
  213.9 32.6 %mlp_both.1 = (bf16[1520,768]{1,0:T(8,128)(2,1)}, bf16[1520,768]{1,0:T(8,128)(2,1)}, f32[1216,768]{1,0:T(8,128)}, f32[1216,1]{1,0:T(8,128)}, f32[1216,192]{1,0:T(8,128)}) custom-call(bf16[1216,768]{1,0:T(8,128)(2,1)} %get-tuple-element.38.n_ref, bf16[1216,768]{1,0:T(8,128)(2,1)} %get-tuple-element.39.gated_ref, bf16[8,4,2,96,768]{4,3,2,1,0:T(8,128)(2,1)} %bitcast.63, ...), custom_call_target="tpu_custom_call" | custom-call | flops 18647875584 | bytes 9437184 | tf_op jit(solution)/shard_map/mlp_both/pallas_call | solution.py:295
  246.4 34.6 %backward_attention.1 = (bf16[1216,2304]{1,0:T(8,128)(2,1)}, f32[1216,768]{1,0:T(8,128)}, bf16[1216,768]{1,0:T(8,128)(2,1)}, f32[1216,1]{1,0:T(8,128)}, f32[8,768]{1,0:T(8,128)}) custom-call(f32[1216,768]{1,0:T(8,128)} %get-tuple-element.41.grad_ref, f32[1216,1]{1,0:T(8,128)} %get-tuple-element.42.gate_part_ref, f32[1216,768]{1,0:T(8,128)} %get-tuple-element.37.hidden_ref, ...), custom_call_target="tpu_custom_call" | custom-call | flops 20082327552 | bytes 18677760 | tf_op jit(solution)/shard_map/backward_attention/pallas_call | solution.py:419
  290.1 11.5 %first_norm.1 = (bf16[1216,768]{1,0:T(8,128)(2,1)}, f32[8,768]{1,0:T(8,128)}) custom-call(bf16[1216,2304]{1,0:T(8,128)(2,1)} %get-tuple-element.46.gproj_ref, bf16[8,4,96,768]{3,2,1,0:T(8,128)(2,1)} %bitcast.58, bf16[1216,768]{1,0:T(8,128)(2,1)} %get-tuple-element.36.x_ref, f32[1216,768]{1,0:T(8,128)} %get-tuple-element.47.ghid_ref, ...), custom_call_target="tpu_custom_call" | custom-call | flops 4303355904 | bytes 14942208 | tf_op jit(solution)/shard_map/first_norm/pallas_call | solution.py:499
  302.3 23.9 %psum.36 = f32[9,768]{1,0:T(8,128)S(1)} all-reduce(f32[9,768]{1,0:T(8,128)S(1)} %pad_maximum_fusion.5), channel_id=1, replica_groups=mesh['rows'=8,'mlp'=4] {'rows'}, use_global_device_ids=true, to_apply=%region_3.4 | all-reduce | flops 6912 | bytes 55296 | tf_op jit(solution)/shard_map/psum | solution.py:726
  327.3 5.0 %fusion.7 = bf16[768,768]{1,0:T(8,128)(2,1)} fusion(bf16[1216,768]{1,0:T(8,128)(2,1)} %get-tuple-element.39.gated_ref, bf16[1520,768]{1,0:T(8,128)(2,1)} %get-tuple-element.55), kind=kOutput, calls=%fused_computation.9 | convolution fusion | flops 1435041792 | bytes 4915200 | tf_op jit(solution)/shard_map/dot_general | solution.py:37
  338.4 4.1 block_out_rows.1
  344.9 9.1 %scatter_rows.1 = bf16[2322,768]{1,0:T(8,128)(2,1)} custom-call(bf16[2322,768]{1,0:T(8,128)(2,1)} %bitcast.59, s32[1,1216]{1,0:T(1,128)} %reshape.89.idx_ref, bf16[1216,768]{1,0:T(8,128)(2,1)} %get-tuple-element.49.rows_ref), custom_call_target="tpu_custom_call" | custom-call | flops 4336975872 | bytes 7133184 | tf_op jit(solution)/shard_map/scatter_rows/pallas_call | solution.py:533
  354.1 56.7 %all-reduce.10.cloned.1.call-done = (bf16[768,576]{0,1:T(8,128)(2,1)}, bf16[192,768]{1,0:T(8,128)(2,1)}, bf16[768,768]{1,0:T(8,128)(2,1)}, bf16[768,768]{1,0:T(8,128)(2,1)}) async-done(((bf16[768,576]{0,1:T(8,128)(2,1)}, bf16[192,768]{1,0:T(8,128)(2,1)}, bf16[768,768]{1,0:T(8,128)(2,1)}, bf16[768,768]{1,0:T(8,128)(2,1)}), (bf16[768,576]{0,1:T(8,128)(2,1)}, bf16[192,768]{1,0:T(8,128)(2,1)}, ...) | async-done | bytes 3538960 | tf_op jit(solution)/shard_map/psum | solution.py:716
  (123 shorter events, 51.9 us)
Async XLA Ops:
  7.2 2.0 copy-start.6
  7.2 138.5 %all-gather.8.cloned.1.call-start = ((), (), s32[]{:S(2)}) async-start(), calls=%async_computation | async-start | bytes 4669440 | tf_op jit(solution)/shard_map/all_gather | solution.py:657
  7.9 152.7 %all-gather.10.cloned.1.call-start = ((), (), s32[]{:S(2)}) async-start(), calls=%async_computation.1 | async-start | bytes 5308416 | tf_op jit(solution)/shard_map/all_gather | solution.py:646
  9.3 8.9 %collective-permute-start = (bf16[96,768]{1,0:T(8,128)(2,1)S(1)}, bf16[96,768]{1,0:T(8,128)(2,1)S(1)}, u32[]{:S(2)}, u32[]{:S(2)}) collective-permute-start(bf16[96,768]{1,0:T(8,128)(2,1)S(1)} %fusion.16), channel_id=1, source_target_pairs={{0,1},{1,2},{2,3},{3,0},{4,5},{5,6},{6,7},{7,4},{8,9},{9,10},{10,1... | collective-permute-start | bytes 442376 | tf_op jit(solution)/shard_map/ppermute | solution.py:576
  18.3 7.2 %collective-permute-start.1 = (bf16[96,768]{1,0:T(8,128)(2,1)S(1)}, bf16[96,768]{1,0:T(8,128)(2,1)S(1)}, u32[]{:S(2)}, u32[]{:S(2)}) collective-permute-start(bf16[96,768]{1,0:T(8,128)(2,1)S(1)} %collective-permute-done), channel_id=1, source_target_pairs={{0,1},{1,2},{2,3},{3,0},{4,5},{5,6},{6,7},{7,4},{8,9},{9,10},{10,1... | collective-permute-start | bytes 442376 | tf_op jit(solution)/shard_map/ppermute | solution.py:576
  25.5 10.7 %collective-permute-start.2 = (bf16[96,768]{1,0:T(8,128)(2,1)S(1)}, bf16[96,768]{1,0:T(8,128)(2,1)S(1)}, u32[]{:S(2)}, u32[]{:S(2)}) collective-permute-start(bf16[96,768]{1,0:T(8,128)(2,1)S(1)} %collective-permute-done.1), channel_id=1, source_target_pairs={{0,1},{1,2},{2,3},{3,0},{4,5},{5,6},{6,7},{7,4},{8,9},{9,10},{10,1... | collective-permute-start | bytes 442376 | tf_op jit(solution)/shard_map/ppermute | solution.py:576
  37.0 171.9 %all-gather.12.cloned.1.call-start = ((), (), s32[]{:S(2)}) async-start(), calls=%async_computation.2 | async-start | bytes 10616832 | tf_op jit(solution)/shard_map/all_gather | solution.py:656
  38.2 60.0 %copy-start.10 = (f32[2,768]{1,0:T(2,128)S(1)}, f32[2,768]{1,0:T(2,128)}, u32[]{:S(2)}) copy-start(f32[2,768]{1,0:T(2,128)} %param.16) | copy-start | bytes 18436
  38.2 60.2 %copy-start.7 = (s32[1461]{0:T(1024)S(1)}, s32[1461]{0:T(1024)}, u32[]{:S(2)}) copy-start(s32[1461]{0:T(1024)} %param.26) | copy-start | bytes 17536
  38.2 16.7 %collective-permute-start.3 = (bf16[2,96,768]{2,1,0:T(8,128)(2,1)S(1)}, bf16[2,96,768]{2,1,0:T(8,128)(2,1)S(1)}, u32[]{:S(2)}, u32[]{:S(2)}) collective-permute-start(bf16[2,96,768]{2,1,0:T(8,128)(2,1)S(1)} %get-tuple-element.66), channel_id=1, source_target_pairs={{0,1},{1,2},{2,3},{3,0},{4,5},{5,6},{6,7},{7,4},{8,9},{9,10},{10,1... | collective-permute-start | bytes 884744 | tf_op jit(solution)/shard_map/ppermute | solution.py:576
  54.9 20.3 %collective-permute-start.4 = (bf16[2,96,768]{2,1,0:T(8,128)(2,1)S(1)}, bf16[2,96,768]{2,1,0:T(8,128)(2,1)S(1)}, u32[]{:S(2)}, u32[]{:S(2)}) collective-permute-start(bf16[2,96,768]{2,1,0:T(8,128)(2,1)S(1)} %collective-permute-done.3), channel_id=1, source_target_pairs={{0,1},{1,2},{2,3},{3,0},{4,5},{5,6},{6,7},{7,4},{8,9},{9,10},{10,1... | collective-permute-start | bytes 884744 | tf_op jit(solution)/shard_map/ppermute | solution.py:576
  75.2 21.6 %collective-permute-start.5 = (bf16[2,96,768]{2,1,0:T(8,128)(2,1)S(1)}, bf16[2,96,768]{2,1,0:T(8,128)(2,1)S(1)}, u32[]{:S(2)}, u32[]{:S(2)}) collective-permute-start(bf16[2,96,768]{2,1,0:T(8,128)(2,1)S(1)} %collective-permute-done.4), channel_id=1, source_target_pairs={{0,1},{1,2},{2,3},{3,0},{4,5},{5,6},{6,7},{7,4},{8,9},{9,10},{10,1... | collective-permute-start | bytes 884744 | tf_op jit(solution)/shard_map/ppermute | solution.py:576
  96.8 6.0 %copy-start.8 = (s32[1461]{0:T(1024)S(1)}, s32[1461]{0:T(1024)}, u32[]{:S(2)}) copy-start(s32[1461]{0:T(1024)} %param.25) | copy-start | bytes 17536
  98.0 7.6 %copy-start.11 = (f32[768]{0:T(1024)S(1)}, f32[768]{0:T(1024)}, u32[]{:S(2)}) copy-start(f32[768]{0:T(1024)} %param.24) | copy-start | bytes 9220
  98.0 8.2 %copy-start.12 = (f32[768]{0:T(1024)S(1)}, f32[768]{0:T(1024)}, u32[]{:S(2)}) copy-start(f32[768]{0:T(1024)} %param.20) | copy-start | bytes 9220
  98.0 312.8 %all-reduce.10.cloned.1.call-start = ((), (), s32[]{:S(2)}) async-start(), calls=%async_computation.3 | async-start | bytes 7077888 | tf_op jit(solution)/shard_map/psum | solution.py:716
  139.4 2.3 copy-start.13
  141.7 3.7 copy-start.4
  284.2 1.7 copy-start
  285.8 1.5 copy-start.14
  290.1 12.2 %copy-start.9 = (f32[8,768]{1,0:T(8,128)S(1)}, f32[8,768]{1,0:T(8,128)}, u32[]{:S(2)}) copy-start(f32[8,768]{1,0:T(8,128)} %get-tuple-element.50) | copy-start | bytes 73732
  327.3 5.6 %copy-start.1 = (f32[1216,192]{1,0:T(8,128)S(1)}, f32[1216,192]{1,0:T(8,128)}, u32[]{:S(2)}) copy-start(f32[1216,192]{1,0:T(8,128)} %get-tuple-element.40) | copy-start | bytes 2801668
  410.8 2.9 copy-start.2
  413.7 1.6 copy-start.3
  (2 other events, 2.9 us)
Sparse Core Ops, SparseCore 0:
  9.6 98.2 all-gather.7
  110.4 37.2 all-gather.9
  150.1 58.8 all-gather.11
  336.4 74.3 all-reduce.9
